TPU v7x, 256 devices: a whole 4x4x8 slice. The times are simulated.
256 devices in a mesh: row: 32 (over y, x, core), col: 8 (over z).
Axes of the slice: x: 4, y: 4, z: 8, core: 2. Of those that a mesh axis runs over, the one named last changes fastest.
Arguments:
- gram: float32 [16384, 16384], P('row', 'col'), may hold values from -70 to 70, as said below
- descriptors: float32 [16384, 2048], P('row', 'col'), may hold values from -0.6 to 0.6
Outputs:
- factored: float32 [16384, 16384], P('row', 'col')
- reduced: float32 [16384, 2048], P('row', 'col')
- variance: float32 [2048], P('col')
Inputs may be any that keep to these rules, and one draw needn't show every extreme that they name: `gram`: symmetric positive definite in natural order with a positive diagonal; columns stored as the steps say.
All inputs are finite; a program needn't handle non-finite values.
Results may differ from a plain program's by a relative error of at most 0.0001.
Values sent between devices are 32-bit elements; how exact they have to be, the bound alone decides.
No kernel may reach another device: no remote copies, remote signals or barrier semaphores. Data moves between devices by JAX's collectives and lax.ppermute only.
A program may use at most 128 MiB of HBM per device.

v0:
```python
import jax
import jax.numpy as jnp
from jax import lax
from jax.sharding import PartitionSpec as P

PANELS = 2


def from_root(block, axis, owner):
    block = jnp.where(lax.axis_index(axis) == owner, block, jnp.zeros_like(block))
    return lax.psum(block, axis)


def body(gram, descriptors):
    width = gram.shape[0]
    stored = gram.shape[1]
    nrow = lax.axis_size("row")
    ncol = lax.axis_size("col")
    blocks = nrow // ncol
    prow = lax.axis_index("row")
    pcol = lax.axis_index("col")
    local = lax.broadcasted_iota(jnp.int32, (width, stored), 1)
    global_col = local // width * (ncol * width) + pcol * width + local % width
    identity = jnp.eye(width, dtype=jnp.float32)
    variance = jnp.zeros((descriptors.shape[1],), jnp.float32)
    for k in range(PANELS):
        panel = gram[:, :width]
        diag = from_root(panel, "row", k)
        factor = jnp.linalg.cholesky(jnp.where(pcol == k, diag, identity))
        solved = jax.scipy.linalg.solve_triangular(factor, panel.T, lower=True).T
        mine = jnp.where(prow < k, 0.0, jnp.where(prow == k, factor, solved))
        mine = jnp.where(pcol == k, mine, 0.0)
        rows_l = from_root(mine, "col", k)
        pivot = jnp.where(prow == k, rows_l, identity)
        solved_x = jax.scipy.linalg.solve_triangular(pivot, descriptors, lower=True)
        part = from_root(solved_x, "row", k)
        lowered = descriptors - jnp.dot(rows_l, part, precision=lax.Precision.HIGHEST)
        descriptors = jnp.where(prow == k, part, jnp.where(prow > k, lowered, descriptors))
        variance = variance + jnp.sum(part * part, axis=0)
        slab = width // ncol
        piece = lax.dynamic_slice_in_dim(rows_l, pcol * slab, slab, 0)
        every = lax.all_gather(piece, "row", axis=0, tiled=True)
        every = every.reshape(blocks, ncol, slab, width)
        moved = lax.all_to_all(every, "col", split_axis=1, concat_axis=2, tiled=True)
        columns = moved.reshape(stored, width)
        update = lax.dot_general(
            rows_l, columns, (((1,), (1,)), ((), ())), precision=lax.Precision.HIGHEST
        )
        gram = gram - update
        gram = gram.at[:, :width].set(jnp.where(pcol == k, rows_l, gram[:, :width]))
        gram = jnp.where((prow == k) & (global_col >= (k + 1) * width), 0.0, gram)
    return (gram, descriptors, variance)


def solution(mesh):
    in_specs = (P("row", "col"), P("row", "col"))
    out_specs = (P("row", "col"), P("row", "col"), P("col"))
    return jax.shard_map(body, mesh=mesh, in_specs=in_specs, out_specs=out_specs, check_vma=False)
```

profile of v0, /device:TPU:9, one launch (start us, length us, event | category | flops | bytes accessed | tf_op | source)
XLA Modules:
  0.0 1299.0 jit_solution(11179091571412308488)
XLA Ops:
  7.2 5.3 copy.70
  12.6 2.9 slice_select_fusion.1
  15.5 117.6 %all-reduce.8.cloned.1.call-done = f32[512,512]{0,1:T(8,128)} async-done(((f32[512,512]{0,1:T(8,128)}), f32[512,512]{0,1:T(8,128)}) %all-reduce.8.cloned.1.call-update) | async-done | bytes 1048592 | tf_op jit(solution)/shard_map/psum | solution.py:11
  133.1 1.4 convert_select_fusion.3
  135.1 11.7 cholesky.286
  147.0 9.8 custom-call.31
  157.6 11.7 cholesky.305
  169.5 9.9 custom-call.32
  179.9 1.5 convolution_subtract_fusion.17
  181.4 11.7 cholesky.326
  193.3 9.8 custom-call.33
  204.7 11.9 cholesky.343
  222.1 10.6 while.10
  232.7 40.7 %custom-call.34 = f32[4,128,128]{1,2,0:T(8,128)} custom-call(f32[4,128,128]{2,1,0:T(8,128)} %get-tuple-element.58), custom_call_target="InvertDiagBlocksLowerTriangular" | custom-call | tf_op jit(solution)/shard_map/jit(_solve_triangular)/triangular_solve | solution.py:30
  281.4 71.6 %all-reduce.10.cloned.1.call-done = f32[512,512]{0,1:T(8,128)} async-done(((f32[512,512]{0,1:T(8,128)}), f32[512,512]{0,1:T(8,128)}) %all-reduce.10.cloned.1.call-update) | async-done | bytes 1048592 | tf_op jit(solution)/shard_map/psum | solution.py:11
  354.8 55.2 %all-gather.3.cloned.1.call-done = f32[2048,512]{1,0:T(8,128)} async-done(((f32[64,512]{1,0:T(8,128)}), f32[2048,512]{1,0:T(8,128)}) %all-gather.3.cloned.1.call-update) | async-done | bytes 4194320 | tf_op jit(solution)/shard_map/all_gather | solution.py:42
  410.1 4.8 copy.68
  414.9 6.7 all-to-all-start
  422.9 95.6 %all-to-all-done = f32[4,8,64,512]{3,2,0,1:T(8,128)} async-done(((f32[4,8,64,512]{3,2,0,1:T(8,128)}), f32[4,8,64,512]{3,2,0,1:T(8,128)}, u32[]{:S(2)}, u32[]{:S(2)}) %all-to-all-start) | async-done | bytes 4194336 | tf_op jit(solution)/shard_map/all_to_all | solution.py:44
  518.5 2.9 copy.69
  521.9 8.3 convolution_subtract_fusion.1
  530.2 3.2 fusion.13
  533.5 8.1 while.12
  541.6 39.3 %custom-call.39 = f32[4,128,128]{1,2,0:T(8,128)S(1)} custom-call(f32[4,128,128]{2,1,0:T(8,128)S(1)} %get-tuple-element.60), custom_call_target="InvertDiagBlocksLowerTriangular" | custom-call | tf_op jit(solution)/shard_map/jit(_solve_triangular)/triangular_solve | solution.py:35
  584.3 6.0 fusion.5
  590.3 2.0 copy-done.1
  592.3 1.6 slice_select_fusion
  594.2 110.2 %all-reduce.16.cloned.1.call-done = (f32[512,512]{0,1:T(8,128)}, f32[512,256]{1,0:T(8,128)}) async-done(((f32[512,512]{0,1:T(8,128)}, f32[512,256]{1,0:T(8,128)}), (f32[512,512]{0,1:T(8,128)}, f32[512,256]{1,0:T(8,128)})) %all-reduce.16.cloned.1.call-update) | async-done | bytes 1572880 | tf_op jit(solution)/shard_map/psum | solution.py:11
  705.9 1.5 fusion.22
  707.3 11.7 cholesky.358
  719.8 9.8 custom-call.35
  730.4 11.7 cholesky.377
  743.5 10.6 custom-call.36
  756.4 1.5 convolution_subtract_fusion.16
  757.9 11.7 cholesky.398
  770.3 9.8 custom-call.37
  781.7 12.1 cholesky.415
  803.0 14.3 %while.11 = (s32[]{:T(128)}, f32[512,512]{0,1:T(8,128)}, s32[4,2]{0,1:T(2,128)S(1)}, f32[4,128,128]{2,1,0:T(8,128)}, s32[]{:T(128)}) while((s32[]{:T(128)}, f32[512,512]{0,1:T(8,128)}, s32[4,2]{0,1:T(2,128)S(1)}, f32[4,128,128]{2,1,0:T(8,128)}, s32[]{:T(128)}) %tuple.135), condition=%wide.while_cond.2.clone, body=%wide.while_body.2.clone.sunk | while | flops 2 | bytes 393329 | solution.py:30
  803.6 2.2 dynamic-slice.41
  807.2 2.2 dynamic-slice.41
  810.8 2.2 dynamic-slice.41
  814.4 2.2 dynamic-slice.41
  817.3 40.7 %custom-call.38 = f32[4,128,128]{1,2,0:T(8,128)} custom-call(f32[4,128,128]{2,1,0:T(8,128)} %get-tuple-element.59), custom_call_target="InvertDiagBlocksLowerTriangular" | custom-call | tf_op jit(solution)/shard_map/jit(_solve_triangular)/triangular_solve | solution.py:30
  864.5 1.6 convolution_subtract_fusion.8
  868.6 72.0 %all-reduce.12.cloned.1.call-done = f32[512,512]{0,1:T(8,128)} async-done(((f32[512,512]{0,1:T(8,128)}), f32[512,512]{0,1:T(8,128)}) %all-reduce.12.cloned.1.call-update) | async-done | bytes 1048592 | tf_op jit(solution)/shard_map/psum | solution.py:11
  942.5 55.1 %all-gather.5.cloned.1.call-done = f32[2048,512]{1,0:T(8,128)} async-done(((f32[64,512]{1,0:T(8,128)}), f32[2048,512]{1,0:T(8,128)}) %all-gather.5.cloned.1.call-update) | async-done | bytes 4194320 | tf_op jit(solution)/shard_map/all_gather | solution.py:42
  997.7 4.8 copy.82
  1002.5 6.9 all-to-all-start.1
  1009.5 1.8 fusion.9
  1011.3 94.9 %all-to-all-done.1 = f32[4,8,64,512]{3,2,0,1:T(8,128)} async-done(((f32[4,8,64,512]{3,2,0,1:T(8,128)}), f32[4,8,64,512]{3,2,0,1:T(8,128)}, u32[]{:S(2)}, u32[]{:S(2)}) %all-to-all-start.1) | async-done | bytes 4194336 | tf_op jit(solution)/shard_map/all_to_all | solution.py:44
  1106.2 2.9 copy.83
  1109.7 8.4 convolution_subtract_fusion
  1118.1 3.5 fusion.12
  1121.7 11.7 while.13
  1122.3 2.2 dynamic-slice.45
  1125.2 2.2 dynamic-slice.45
  1128.1 2.2 dynamic-slice.45
  1131.1 2.1 dynamic-slice.45
  1133.4 39.3 %custom-call.40 = f32[4,128,128]{1,2,0:T(8,128)S(1)} custom-call(f32[4,128,128]{2,1,0:T(8,128)S(1)} %get-tuple-element.61), custom_call_target="InvertDiagBlocksLowerTriangular" | custom-call | tf_op jit(solution)/shard_map/jit(_solve_triangular)/triangular_solve | solution.py:35
  1176.1 1.4 convolution_subtract_fusion.12
  1178.7 7.6 fusion.3
  1186.3 5.3 copy.87
  1191.6 94.9 %all-reduce.14.cloned.1.call-done = f32[512,256]{1,0:T(8,128)} async-done(((f32[512,256]{1,0:T(8,128)}), f32[512,256]{1,0:T(8,128)}) %all-reduce.14.cloned.1.call-update) | async-done | bytes 524304 | tf_op jit(solution)/shard_map/psum | solution.py:11
  1288.2 3.8 fusion.7
  (235 shorter events, 81.8 us)
Async XLA Ops:
  7.2 125.9 %all-reduce.8.cloned.1.call-start = ((), (), s32[]{:S(2)}) async-start(), calls=%async_computation.2 | async-start | bytes 2097152 | tf_op jit(solution)/shard_map/psum | solution.py:11
  15.5 337.5 %all-reduce.10.cloned.1.call-start = ((), (), s32[]{:S(2)}) async-start(), calls=%async_computation.3 | async-start | bytes 2097152 | tf_op jit(solution)/shard_map/psum | solution.py:11
  133.1 1.8 copy-start.6
  135.1 34.4 %copy-start.9 = (f32[512,512]{1,0:T(8,128)}, f32[512,512]{1,0:T(8,128)S(1)}, u32[]{:S(2)}) copy-start(f32[512,512]{1,0:T(8,128)S(1)} %fusion.23) | copy-start | bytes 3145732
  179.4 94.0 %copy-start.7 = (f32[512,512]{1,0:T(8,128)S(1)}, f32[512,512]{1,0:T(8,128)}, u32[]{:S(2)}) copy-start(f32[512,512]{1,0:T(8,128)} %get-tuple-element.164) | copy-start | bytes 3145732
  281.3 128.7 %all-gather.3.cloned.1.call-start = ((), (), s32[]{:S(2)}) async-start(), calls=%async_computation.4 | async-start | bytes 4325376 | tf_op jit(solution)/shard_map/all_gather | solution.py:42
  414.9 103.6 %all-to-all-start = ((f32[4,8,64,512]{3,2,0,1:T(8,128)}), f32[4,8,64,512]{3,2,0,1:T(8,128)}, u32[]{:S(2)}, u32[]{:S(2)}) async-start(f32[4,8,64,512]{3,2,0,1:T(8,128)} %copy.68), calls=%async_computation | async-start | bytes 8388608 | tf_op jit(solution)/shard_map/all_to_all | solution.py:44
  421.6 282.7 %all-reduce.16.cloned.1.call-start = ((), (), s32[]{:S(2)}) async-start(), calls=%async_computation.8 | async-start | bytes 3145728 | tf_op jit(solution)/shard_map/psum | solution.py:11
  422.8 161.4 %copy-start.21 = (pred[2048]{0:T(1024)(128)(4,1)}, pred[2048]{0:T(1024)(128)(4,1)S(1)}, u32[]{:S(2)}) copy-start(pred[2048]{0:T(1024)(128)(4,1)S(1)} %get-tuple-element.188) | copy-start | bytes 6148
  422.8 161.4 %copy-start.15 = (s32[2048]{0:T(1024)}, s32[2048]{0:T(1024)S(1)}, u32[]{:S(2)}) copy-start(s32[2048]{0:T(1024)S(1)} %get-tuple-element.186) | copy-start | bytes 24580
  422.9 161.4 %copy-start.17 = (s32[2048]{0:T(1024)}, s32[2048]{0:T(1024)S(1)}, u32[]{:S(2)}) copy-start(s32[2048]{0:T(1024)S(1)} %get-tuple-element.183) | copy-start | bytes 24580
  422.9 161.4 %copy-start.19 = (s32[2048]{0:T(1024)}, s32[2048]{0:T(1024)S(1)}, u32[]{:S(2)}) copy-start(s32[2048]{0:T(1024)S(1)} %get-tuple-element.184) | copy-start | bytes 24580
  422.9 98.5 %copy-start.3 = (f32[512,512]{0,1:T(8,128)S(1)}, f32[512,512]{0,1:T(8,128)}, u32[]{:S(2)}) copy-start(f32[512,512]{0,1:T(8,128)} %all-reduce.10.cloned.1.call-done) | copy-start | bytes 3145732
  518.5 3.4 copy-start
  530.2 50.7 %copy-start.11 = (f32[512,256]{1,0:T(8,128)S(1)}, f32[512,256]{1,0:T(8,128)}, u32[]{:S(2)}) copy-start(f32[512,256]{1,0:T(8,128)} %param.12) | copy-start | bytes 1572868
  590.3 2.0 copy-start.1
  593.9 346.7 %all-reduce.12.cloned.1.call-start = ((), (), s32[]{:S(2)}) async-start(), calls=%async_computation.5 | async-start | bytes 2097152 | tf_op jit(solution)/shard_map/psum | solution.py:11
  704.4 1.5 copy-start.5
  707.3 36.1 %copy-start.10 = (f32[512,512]{1,0:T(8,128)}, f32[512,512]{1,0:T(8,128)S(1)}, u32[]{:S(2)}) copy-start(f32[512,512]{1,0:T(8,128)S(1)} %fusion.22) | copy-start | bytes 3145732
  730.2 13.2 %copy-start.14 = (f32[384,128]{1,0:T(8,128)}, f32[384,128]{1,0:T(8,128)S(1)}, u32[]{:S(2)}) copy-start(f32[384,128]{1,0:T(8,128)S(1)} %convolution_subtract_fusion.10) | copy-start | bytes 589828
  754.1 104.0 %copy-start.8 = (f32[512,512]{1,0:T(8,128)S(1)}, f32[512,512]{1,0:T(8,128)}, u32[]{:S(2)}) copy-start(f32[512,512]{1,0:T(8,128)} %get-tuple-element.162) | copy-start | bytes 3145732
  868.6 129.1 %all-gather.5.cloned.1.call-start = ((), (), s32[]{:S(2)}) async-start(), calls=%async_computation.6 | async-start | bytes 4325376 | tf_op jit(solution)/shard_map/all_gather | solution.py:42
  1002.5 6.9 copy-start.13
  1002.5 7.0 copy-start.12
  1002.5 103.7 %all-to-all-start.1 = ((f32[4,8,64,512]{3,2,0,1:T(8,128)}), f32[4,8,64,512]{3,2,0,1:T(8,128)}, u32[]{:S(2)}, u32[]{:S(2)}) async-start(f32[4,8,64,512]{3,2,0,1:T(8,128)} %copy.82), calls=%async_computation.1 | async-start | bytes 8388608 | tf_op jit(solution)/shard_map/all_to_all | solution.py:44
  1009.4 277.2 %all-reduce.14.cloned.1.call-start = ((), (), s32[]{:S(2)}) async-start(), calls=%async_computation.7 | async-start | bytes 1048576 | tf_op jit(solution)/shard_map/psum | solution.py:11
  1011.3 97.8 %copy-start.4 = (f32[512,512]{0,1:T(8,128)S(1)}, f32[512,512]{0,1:T(8,128)}, u32[]{:S(2)}) copy-start(f32[512,512]{0,1:T(8,128)} %all-reduce.12.cloned.1.call-done) | copy-start | bytes 3145732
  1106.2 3.4 copy-start.2
  1121.6 57.1 %copy-start.16 = (s32[2048]{0:T(1024)S(1)}, s32[2048]{0:T(1024)}, u32[]{:S(2)}) copy-start(s32[2048]{0:T(1024)} %copy-done.15) | copy-start | bytes 24580
  1121.6 57.1 %copy-start.18 = (s32[2048]{0:T(1024)S(1)}, s32[2048]{0:T(1024)}, u32[]{:S(2)}) copy-start(s32[2048]{0:T(1024)} %copy-done.17) | copy-start | bytes 24580
  1121.6 57.1 %copy-start.20 = (s32[2048]{0:T(1024)S(1)}, s32[2048]{0:T(1024)}, u32[]{:S(2)}) copy-start(s32[2048]{0:T(1024)} %copy-done.19) | copy-start | bytes 24580
  1121.6 57.1 %copy-start.22 = (pred[2048]{0:T(1024)(128)(4,1)S(1)}, pred[2048]{0:T(1024)(128)(4,1)}, u32[]{:S(2)}) copy-start(pred[2048]{0:T(1024)(128)(4,1)} %copy-done.21) | copy-start | bytes 6148
Sparse Core Ops, SparseCore 0:
  15.6 117.4 all-reduce.7
  281.5 71.4 all-reduce.9
  356.4 53.5 all-gather.2
  594.0 110.2 all-reduce.15
  868.7 71.8 all-reduce.11
  943.6 53.9 all-gather.4
  1178.8 107.6 all-reduce.13
where the time goes:
time: 1310 us; the launch traced here: 1300 us
  waiting for transfers between devices  767 us (59%)
  other arithmetic  359 us (27%)
  local copies, waits for them, and re-layouts  83.3 us (6%)
  matrix products  54.8 us (4%)
  between operations  20.2 us (2%)
  starting transfers between devices  14.4 us (1%)
    psum x5, waiting for transfers between devices, from_root(): return lax.psum(block, axis)  466 us
    all_to_all x2, waiting for transfers between devices, body(): lax.all_to_all(every, 'col', split_axis=1, concat_axis=2, tiled=True)  190 us
    another operation x29, other arithmetic, body(): factor = jnp.linalg.cholesky(jnp.where(pcol == k, diag, identity))  163 us
    all_gather x2, waiting for transfers between devices, body(): every = lax.all_gather(piece, 'row', axis=0, tiled=True)  110 us
    another operation x4, other arithmetic, body(): solved_x = jax.scipy.linalg.solve_triangular(pivot, descriptors, lower=True)  85.4 us
    another operation x5, other arithmetic, body(): solved = jax.scipy.linalg.solve_triangular(factor, panel.T, lower=True).T  82.8 us
    another operation x45, local copies, waits for them, and re-layouts, body(): solved = jax.scipy.linalg.solve_triangular(factor, panel.T, lower=True).T  26.2 us
  transfers between devices with their start and end apart: 9, of which 9 were waited for; matrix products, arithmetic and copies ran while one was open for 1% of the time, Pallas kernels for 0%

commit v1 on v0

v1 whole, which is shorter than its diff:
```python
import jax
import jax.numpy as jnp
from jax import lax
from jax.experimental import pallas as pl
from jax.experimental.pallas import tpu as pltpu
from jax.sharding import PartitionSpec as P

HIGHEST = lax.Precision.HIGHEST
HIGH = lax.Precision.HIGH
TILE = 128
SUB = 8


def lane_of(x, at):
    return jnp.broadcast_to(x[:, at:at + 1], x.shape)


def sub_of(x, at):
    return jnp.broadcast_to(x[at:at + 1, :], x.shape)


def invert_tile(rows):
    shape = rows[0].shape
    lane = lax.broadcasted_iota(jnp.int32, shape, 1)
    sub = lax.broadcasted_iota(jnp.int32, shape, 0)
    count = len(rows)
    for p in range(count):
        at = SUB * p
        panel = (lane >= at) & (lane < at + SUB)
        row = rows[p]
        diag = [lane_of(row, at + k) for k in range(SUB)]
        row = jnp.where(panel, jnp.where(lane == sub + at, 1.0, 0.0), row)
        inv, tops, low = [], [], {}
        for k in range(SUB):
            scale = lax.rsqrt(sub_of(diag[k], k))
            inv.append(scale)
            mult = diag[k] * scale
            top = sub_of(row, k) * scale
            tops.append(top)
            for j in range(k + 1, SUB):
                low[j, k] = sub_of(diag[j], k) * scale
                diag[j] = diag[j] - mult * low[j, k]
            row = row - mult * top
        done = tops[0]
        for k in range(1, SUB):
            done = jnp.where(sub == k, tops[k], done)
        rows[p] = jnp.where(lane <= sub + at, done, 0.0)
        for i in range(p + 1, count):
            cols = [lane_of(rows[i], at + k) for k in range(SUB)]
            rest = jnp.where(panel, 0.0, rows[i])
            for k in range(SUB):
                mult = cols[k] * inv[k]
                for j in range(k + 1, SUB):
                    cols[j] = cols[j] - mult * low[j, k]
                rest = rest - mult * tops[k]
            rows[i] = rest
    return jnp.concatenate(rows, axis=0)


def factor_kernel(a_ref, t_ref):
    count = a_ref.shape[0] // TILE
    t_ref[...] = a_ref[...]

    def block(i):
        return pl.ds(pl.multiple_of(i * TILE, TILE), TILE)

    def step(j, carry):
        here = block(j)
        rows = [
            t_ref[pl.ds(pl.multiple_of(j * TILE + SUB * i, SUB), SUB), here]
            for i in range(TILE // SUB)
        ]
        tile = invert_tile(rows)
        t_ref[here, :] = jnp.dot(tile, t_ref[here, :], precision=HIGHEST)
        lefts = t_ref[here, :]
        t_ref[here, here] = tile

        def below(i, carry):
            there = block(i)
            left = t_ref[here, there]
            t_ref[there, here] = jnp.zeros((TILE, TILE), jnp.float32)
            t_ref[there, :] -= lax.dot_general(
                left, t_ref[here, :], (((0,), (0,)), ((), ())), precision=HIGHEST,
                preferred_element_type=jnp.float32,
            )
            return carry

        return lax.fori_loop(j + 1, count, below, carry)

    lax.fori_loop(0, count, step, 0)


def factor_inverse(a):
    order = a.shape[0]
    return pl.pallas_call(
        factor_kernel,
        out_shape=jax.ShapeDtypeStruct(a.shape, jnp.float32),
        in_specs=[pl.BlockSpec(memory_space=pltpu.VMEM)],
        out_specs=pl.BlockSpec(memory_space=pltpu.VMEM),
        compiler_params=pltpu.CompilerParams(vmem_limit_bytes=40 * 2**20),
        cost_estimate=pl.CostEstimate(flops=6 * order**3, bytes_accessed=8 * order * order, transcendentals=order),
        name="factor_inverse",
    )(a)


def mesh_shapes():
    return lax.axis_size("row"), lax.axis_size("col")


def body(gram, desc):
    nb = gram.shape[0]
    stored = gram.shape[1]
    nrow, ncol = mesh_shapes()
    groups = nrow // ncol
    order = 2 * nb
    prow = lax.axis_index("row")
    pcol = lax.axis_index("col")
    slab = nb // ncol
    panel = gram[:, :nb]

    got = lax.all_to_all(panel.reshape(ncol, slab, nb), "col", 0, 0, tiled=True)
    rows_slab = jnp.concatenate([got[0], got[1]], axis=1)

    tiles = rows_slab.reshape(slab // 8, 8, order // 256, 256).transpose(0, 2, 1, 3)
    tiles = tiles.reshape(nrow, 8, 256)
    dealt = lax.all_to_all(tiles, "row", 0, 0, tiled=True)[:2]
    lead = lax.all_gather(dealt, "col")
    lead = lax.all_to_all(
        jnp.broadcast_to(lead[None], (nrow,) + lead.shape), "row", 0, 0, tiled=True
    )
    lead = lead.reshape(slab // 8, order // 256, ncol, 2, 8, 256)
    lead = lead.transpose(3, 2, 0, 4, 1, 5).reshape(order, order)

    mine = lax.all_gather(rows_slab, "col", tiled=True)
    halves = [None, None]
    inner = prow % ncol
    pieces = panel.reshape(ncol, slab, nb)
    got0 = jnp.zeros((slab, nb), jnp.float32)
    got1 = jnp.zeros((slab, nb), jnp.float32)
    for s in range(ncol):
        pairs = []
        for y in range(groups):
            for i in range(ncol):
                pairs.append(((y * ncol + i) * ncol, (y * ncol + (i + s) % ncol) * ncol + i))
                pairs.append(
                    ((y * ncol + i) * ncol + 1, (y * ncol + (i + s + ncol // 2) % ncol) * ncol + i)
                )
        which = (inner + s + jnp.where(pcol == 0, 0, ncol // 2)) % ncol
        piece = lax.dynamic_index_in_dim(pieces, which, 0, keepdims=False)
        come = lax.ppermute(piece, ("row", "col"), pairs)
        got0 = jnp.where((inner - pcol - s) % ncol == 0, come, got0)
        got1 = jnp.where((inner - pcol - s - ncol // 2) % ncol == 0, come, got1)
    match = lax.all_gather(jnp.concatenate([got0, got1], axis=1), "row", tiled=True)

    chunk = desc.shape[0] // nrow
    head = lax.all_to_all(desc.reshape(nrow, chunk, -1), "row", 0, 0, tiled=True)[:2]
    head = lax.all_gather(head, "row")
    head = head.transpose(1, 0, 2, 3).reshape(order, -1)

    inverse = factor_inverse(lead)
    lower = jnp.where(
        lax.broadcasted_iota(jnp.int32, (order, order), 0)
        >= lax.broadcasted_iota(jnp.int32, (order, order), 1),
        inverse, 0.0,
    )
    solved = lax.dot_general(mine, lower, (((1,), (1,)), ((), ())), precision=HIGHEST)
    weights = jnp.dot(solved, lower, precision=HIGHEST)
    update = lax.dot_general(weights, match, (((1,), (1,)), ((), ())), precision=HIGH)
    z = jnp.dot(lower, head, precision=HIGHEST)
    variance = jnp.sum(z * z, axis=0)
    lowered = desc - jnp.dot(weights, head, precision=HIGH)
    reduced = jnp.where(prow == 0, z[:nb], jnp.where(prow == 1, z[nb:], lowered))

    row_at = prow * nb + lax.broadcasted_iota(jnp.int32, (nb, nb), 0)
    col_at = pcol * nb + lax.broadcasted_iota(jnp.int32, (nb, nb), 1)
    factor = jnp.where(pcol == 0, solved[:, :nb], solved[:, nb:])
    factor = jnp.where(row_at >= col_at, factor, 0.0)
    rest = jnp.where(prow < 2, 0.0, gram - update)
    rest = rest.at[:, :nb].set(jnp.where(pcol < 2, factor, rest[:, :nb]))
    return (rest, reduced, variance)


def solution(mesh):
    in_specs = (P("row", "col"), P("row", "col"))
    out_specs = (P("row", "col"), P("row", "col"), P("col"))
    return jax.shard_map(body, mesh=mesh, in_specs=in_specs, out_specs=out_specs, check_vma=False)
```

time: 1310 us -> 343 us (0.26)
  waiting for transfers between devices: 767 us -> 101 us
  other arithmetic: 359 us -> 3.44 us
  blocking collectives: 0 us -> 67.7 us
  local copies, waits for them, and re-layouts: 83.3 us -> 16.3 us
  Pallas kernels: 0 us -> 55.2 us
  starting transfers between devices: 14.4 us -> 45.9 us
  matrix products: 54.8 us -> 34.5 us
    psum x5 -> x0, waiting for transfers between devices: 466 us -> none  [from_root(): return lax.psum(block, axis)]
    another operation x39 -> x1, other arithmetic: 331 us -> 0.72 us  [the longest x29 163 us: body(): factor = jnp.linalg.cholesky(jnp.where(pcol == k, diag, identity))]
    all_gather x2 -> x3, waiting for transfers between devices: 110 us -> 0.01 us  [the longest x1 0.01 us: body(): head = lax.all_gather(head, 'row')]
    all_to_all x2 -> x3, waiting for transfers between devices: 190 us -> 99.6 us  [the longest x1 63.1 us: body(): lax.all_to_all(jnp.broadcast_to(lead[None], (nrow,) + lead.shape), 'row',...]
    pallas_call x0 -> x1, Pallas kernels: none -> 55.2 us  [factor_inverse(): pl.pallas_call(factor_kernel, out_shape=jax.ShapeDtypeStruct(a.shape, jnp...]
    another operation x111 -> x0, local copies, waits for them, and re-layouts: 48.7 us -> none  [the longest x45 26.2 us: body(): solved = jax.scipy.linalg.solve_triangular(factor, panel.T, lower=True).T]
    all_to_all x0 -> x1, blocking collectives: none -> 46.7 us  [body(): dealt = lax.all_to_all(tiles, 'row', 0, 0, tiled=True)[:2]]
    another operation x40 -> x0, matrix products: 32.4 us -> none  [the longest x14 15.9 us: body(): solved = jax.scipy.linalg.solve_triangular(factor, panel.T, lower=True).T]
  transfers between devices with their start and end apart: 9 -> 14, of which waited for: 9 -> 4; matrix products, arithmetic and copies ran while one was open for 1% -> 11% of each run, Pallas kernels for 0% -> 16%
where the time goes in v1:
time: 343 us; the launch traced here: 339 us
  waiting for transfers between devices  101 us (29%)
  blocking collectives  67.7 us (20%)
  Pallas kernels  55.2 us (16%)
  starting transfers between devices  45.9 us (13%)
  matrix products  34.5 us (10%)
  local copies, waits for them, and re-layouts  16.3 us (5%)
  between operations  14.5 us (4%)
  other arithmetic  3.44 us (1%)
    all_to_all x1, waiting for transfers between devices, body(): lax.all_to_all(jnp.broadcast_to(lead[None], (nrow,) + lead.shape), 'row',...  63.1 us
    pallas_call x1, Pallas kernels, factor_inverse(): pl.pallas_call(factor_kernel, out_shape=jax.ShapeDtypeStruct(a.shape, jnp...  55.2 us
    all_to_all x1, blocking collectives, body(): dealt = lax.all_to_all(tiles, 'row', 0, 0, tiled=True)[:2]  46.7 us
    all_to_all x1, waiting for transfers between devices, body(): got = lax.all_to_all(panel.reshape(ncol, slab, nb), 'col', 0, 0, tiled=True)  28.5 us
    all_gather x1, blocking collectives, body(): lead = lax.all_gather(dealt, 'col')  21 us
    ppermute x8, starting transfers between devices, body(): come = lax.ppermute(piece, ('row', 'col'), pairs)  18.1 us
    all_to_all x1, starting transfers between devices, body(): lax.all_to_all(jnp.broadcast_to(lead[None], (nrow,) + lead.shape), 'row',...  11.6 us
    dot_general x1, matrix products, body(): lax.dot_general(weights, match, (((1,), (1,)), ((), ())), precision=HIGH)  10.7 us
  transfers between devices with their start and end apart: 14, of which 4 were waited for; matrix products, arithmetic and copies ran while one was open for 11% of the time, Pallas kernels for 16%

profile of v1, /device:TPU:9, one launch (start us, length us, event | category | flops | bytes accessed | tf_op | source)
XLA Modules:
  0.0 338.9 jit_solution(2191924419659822813)
XLA Ops:
  7.2 7.9 %all-to-all-start.3 = ((f32[32,16,256]{2,1,0:T(8,128)}), f32[32,16,256]{2,1,0:T(8,128)S(1)}, u32[]{:S(2)}, u32[]{:S(2)}) async-start(f32[32,16,256]{2,1,0:T(8,128)} %bitcast.47), calls=%async_computation.3 | async-start | bytes 1048576 | tf_op jit(solution)/shard_map/all_to_all | solution.py:156
  15.0 2.3 slice.47
  17.3 8.1 %all-to-all-done.3 = f32[32,16,256]{2,1,0:T(8,128)S(1)} async-done(((f32[32,16,256]{2,1,0:T(8,128)}), f32[32,16,256]{2,1,0:T(8,128)S(1)}, u32[]{:S(2)}, u32[]{:S(2)}) %all-to-all-start.3) | async-done | bytes 524320 | tf_op jit(solution)/shard_map/all_to_all | solution.py:156
  25.4 8.2 %all-to-all-start = ((f32[8,64,512]{2,1,0:T(8,128)}), f32[8,64,512]{2,1,0:T(8,128)S(1)}, u32[]{:S(2)}, u32[]{:S(2)}) async-start(f32[8,64,512]{2,1,0:T(8,128)} %bitcast), calls=%async_computation | async-start | bytes 2097152 | tf_op jit(solution)/shard_map/all_to_all | solution.py:121
  33.6 0.0 all-gather.10.cloned.1.call-start
  33.6 0.6 slice.63
  34.2 0.1 all-gather.10.cloned.1.call-update
  34.3 0.0 all-gather.6.cloned.1.call-start
  34.3 28.5 %all-to-all-done = f32[8,64,512]{2,1,0:T(8,128)S(1)} async-done(((f32[8,64,512]{2,1,0:T(8,128)}), f32[8,64,512]{2,1,0:T(8,128)S(1)}, u32[]{:S(2)}, u32[]{:S(2)}) %all-to-all-start) | async-done | bytes 1048608 | tf_op jit(solution)/shard_map/all_to_all | solution.py:121
  62.9 0.7 pad_maximum_fusion
  63.6 0.0 copy-start.4
  63.6 0.0 all-gather.6.cloned.1.call-update
  63.6 0.0 all-gather.8.cloned.1.call-start
  63.9 1.4 dynamic-slice_bitcast_fusion
  65.3 1.8 collective-permute-start.7
  67.1 4.5 %collective-permute-start.6 = (f32[64,512]{1,0:T(8,128)S(1)}, f32[64,512]{1,0:T(8,128)S(1)}, u32[]{:S(2)}, u32[]{:S(2)}) collective-permute-start(f32[64,512]{1,0:T(8,128)S(1)} %get-tuple-element.16), channel_id=1, source_target_pairs={{0,8},{1,40},{8,17},{9,49},{16,26},{17,58},{24,35},{25,3},{32,44},... | collective-permute-start | bytes 393224 | tf_op jit(solution)/shard_map/ppermute | solution.py:150
  71.6 1.3 collective-permute-start.5
  72.9 2.3 collective-permute-start.4
  75.2 1.3 collective-permute-start.3
  76.5 0.0 collective-permute-done.7
  76.6 2.6 collective-permute-start.2
  79.2 0.0 collective-permute-done.6
  79.2 1.3 collective-permute-start.1
  80.5 0.0 collective-permute-done.5
  80.5 2.9 collective-permute-start
  83.7 0.0 collective-permute-done.4
  83.7 0.0 collective-permute-done.3
  83.7 0.0 collective-permute-done.2
  83.7 0.0 collective-permute-done.1
  83.7 1.6 collective-permute-done
  85.4 0.1 select_select_fusion.1
  85.5 0.1 select_select_fusion.2
  85.6 0.8 pad_maximum_fusion.1
  86.3 0.0 all-gather.8.cloned.1.call-update
  86.4 0.0 copy-done.4
  86.4 46.7 %all_to_all.20 = f32[32,8,256]{2,1,0:T(8,128)S(1)} all-to-all(f32[32,8,256]{2,1,0:T(8,128)S(1)} %bitcast.46), channel_id=1, replica_groups=mesh['row'=32,'col'=8] {'row'}, dimensions={0} | all-to-all | bytes 524288 | tf_op jit(solution)/shard_map/all_to_all | solution.py:126
  133.1 21.0 %all-gather = f32[16,8,256]{2,1,0:T(8,128)S(1)} all-gather(f32[2,8,256]{2,1,0:T(8,128)S(1)} %slice.59), channel_id=2, replica_groups=mesh['row'=32,'col'=8] {'col'}, dimensions={0}, use_global_device_ids=true | all-gather | bytes 147456 | tf_op jit(solution)/shard_map/all_gather | solution.py:127
  154.1 2.5 broadcast_in_dim.19
  156.6 11.6 %all-to-all-start.2 = ((f32[32,8,2,8,256]{4,3,1,2,0:T(8,128)}), f32[32,8,2,8,256]{4,3,1,2,0:T(8,128)}, u32[]{:S(2)}, u32[]{:S(2)}) async-start(f32[32,8,2,8,256]{4,3,1,2,0:T(8,128)} %broadcast_in_dim.19), calls=%async_computation.2 | async-start | bytes 8388608 | tf_op jit(solution)/shard_map/all_to_all | solution.py:128
  168.3 0.7 compare_reduce_fusion
  169.0 0.0 all-gather.10.cloned.1.call-done
  169.0 1.3 copy.10
  170.3 63.1 %all-to-all-done.2 = f32[32,8,2,8,256]{4,3,1,2,0:T(8,128)} async-done(((f32[32,8,2,8,256]{4,3,1,2,0:T(8,128)}), f32[32,8,2,8,256]{4,3,1,2,0:T(8,128)}, u32[]{:S(2)}, u32[]{:S(2)}) %all-to-all-start.2) | async-done | bytes 4194336 | tf_op jit(solution)/shard_map/all_to_all | solution.py:128
  233.4 2.8 copy.9
  236.2 55.2 %factor_inverse.1 = f32[1024,1024]{1,0:T(8,128)S(1)} custom-call(f32[1024,1024]{1,0:T(8,128)S(1)} %bitcast.43), custom_call_target="tpu_custom_call" | custom-call | flops 6442450944 | bytes 8388608 | tf_op jit(solution)/shard_map/factor_inverse/pallas_call | solution.py:95
  291.4 0.0 copy-start
  291.4 2.0 copy-done
  293.4 5.0 %multiply_reduce_fusion = (f32[256]{0:T(256)}, f32[1024,256]{1,0:T(8,128)}) fusion(f32[1024,256]{1,0:T(8,128)S(1)} %bitcast.44, f32[1024,1024]{1,0:T(8,128)S(1)} %factor_inverse.1), kind=kOutput, calls=%fused_computation.16 | convolution fusion | flops 3223846656 | bytes 6292480 | tf_op jit(solution)/shard_map/dot_general | solution.py:169
  298.4 0.0 all-gather.6.cloned.1.call-done
  298.4 0.0 copy-start.1
  298.4 10.2 %fusion.5 = f32[512,1024]{1,0:T(8,128)S(1)} fusion(f32[512,1024]{1,0:T(8,128)} %all-gather.6.cloned.1.call-done, f32[1024,1024]{1,0:T(8,128)} %copy-done), kind=kOutput, calls=%fused_computation.5 | convolution fusion | flops 6444548096 | bytes 8388608 | tf_op jit(solution)/shard_map/dot_general | solution.py:166
  308.6 0.0 copy-done.1
  308.6 0.0 copy-start.5
  308.6 0.0 copy-start.6
  308.7 6.8 %fusion.3 = f32[512,1024]{1,0:T(8,128)S(1)} fusion(f32[512,1024]{1,0:T(8,128)S(1)} %fusion.5, f32[1024,1024]{1,0:T(8,128)S(1)} %copy-done.1), kind=kOutput, calls=%fused_computation.4 | convolution fusion | flops 6444548096 | bytes 8388608 | tf_op jit(solution)/shard_map/dot_general | solution.py:167
  315.5 0.0 copy-start.2
  315.5 1.3 copy-done.2
  316.8 0.0 copy-done.5
  316.8 0.0 copy-done.6
  316.8 1.8 fusion.11
  318.6 10.7 %subtract_select_fusion = f32[512,2048]{1,0:T(8,128)S(1)} fusion(f32[512,2048]{1,0:T(8,128)} %param.4, f32[512,1024]{1,0:T(8,128)} %copy-done.2, f32[2048,1024]{1,0:T(8,128)} %all-gather.8.cloned.1.call-done, pred[]{:T(512)S(6)} %lt.125), kind=kOutput, calls=%fused_computation | convolution fusion | flops 6444548096 | bytes 18874368 | tf_op jit(solution)/shard_map/dot_general | solution.py:168
  329.3 1.1 fusion.12
  330.4 0.0 copy-start.3
  330.4 2.0 copy-done.3
  (5 shorter events, 0.0 us)
Async XLA Ops:
  7.2 18.2 %all-to-all-start.3 = ((f32[32,16,256]{2,1,0:T(8,128)}), f32[32,16,256]{2,1,0:T(8,128)S(1)}, u32[]{:S(2)}, u32[]{:S(2)}) async-start(f32[32,16,256]{2,1,0:T(8,128)} %bitcast.47), calls=%async_computation.3 | async-start | bytes 1048576 | tf_op jit(solution)/shard_map/all_to_all | solution.py:156
  25.4 37.5 %all-to-all-start = ((f32[8,64,512]{2,1,0:T(8,128)}), f32[8,64,512]{2,1,0:T(8,128)S(1)}, u32[]{:S(2)}, u32[]{:S(2)}) async-start(f32[8,64,512]{2,1,0:T(8,128)} %bitcast), calls=%async_computation | async-start | bytes 2097152 | tf_op jit(solution)/shard_map/all_to_all | solution.py:121
  33.6 135.4 %all-gather.10.cloned.1.call-start = ((), (), s32[]{:S(2)}) async-start(), calls=%async_computation.6 | async-start | bytes 1081344 | tf_op jit(solution)/shard_map/all_gather | solution.py:157
  34.3 264.1 %all-gather.6.cloned.1.call-start = ((), (), s32[]{:S(2)}) async-start(), calls=%async_computation.4 | async-start | bytes 2359296 | tf_op jit(solution)/shard_map/all_gather | solution.py:134
  63.6 22.8 %copy-start.4 = (f32[64,1024]{1,0:T(8,128)S(1)}, f32[64,1024]{1,0:T(8,128)}, u32[]{:S(2)}) copy-start(f32[64,1024]{1,0:T(8,128)} %pad_maximum_fusion) | copy-start | bytes 786436
  63.6 255.0 %all-gather.8.cloned.1.call-start = ((), (), s32[]{:S(2)}) async-start(), calls=%async_computation.5 | async-start | bytes 8650752 | tf_op jit(solution)/shard_map/all_gather | solution.py:153
  65.3 11.3 %collective-permute-start.7 = (f32[64,512]{1,0:T(8,128)S(1)}, f32[64,512]{1,0:T(8,128)S(1)}, u32[]{:S(2)}, u32[]{:S(2)}) collective-permute-start(f32[64,512]{1,0:T(8,128)S(1)} %get-tuple-element.15), channel_id=1, source_target_pairs={{0,0},{1,32},{8,9},{9,41},{16,18},{17,50},{24,27},{25,59},{32,36},... | collective-permute-start | bytes 393224 | tf_op jit(solution)/shard_map/ppermute | solution.py:150
  67.1 12.1 %collective-permute-start.6 = (f32[64,512]{1,0:T(8,128)S(1)}, f32[64,512]{1,0:T(8,128)S(1)}, u32[]{:S(2)}, u32[]{:S(2)}) collective-permute-start(f32[64,512]{1,0:T(8,128)S(1)} %get-tuple-element.16), channel_id=1, source_target_pairs={{0,8},{1,40},{8,17},{9,49},{16,26},{17,58},{24,35},{25,3},{32,44},... | collective-permute-start | bytes 393224 | tf_op jit(solution)/shard_map/ppermute | solution.py:150
  71.6 8.9 %collective-permute-start.5 = (f32[64,512]{1,0:T(8,128)S(1)}, f32[64,512]{1,0:T(8,128)S(1)}, u32[]{:S(2)}, u32[]{:S(2)}) collective-permute-start(f32[64,512]{1,0:T(8,128)S(1)} %get-tuple-element.17), channel_id=1, source_target_pairs={{0,16},{1,48},{8,25},{9,57},{16,34},{17,2},{24,43},{25,11},{32,52}... | collective-permute-start | bytes 393224 | tf_op jit(solution)/shard_map/ppermute | solution.py:150
  72.9 10.8 %collective-permute-start.4 = (f32[64,512]{1,0:T(8,128)S(1)}, f32[64,512]{1,0:T(8,128)S(1)}, u32[]{:S(2)}, u32[]{:S(2)}) collective-permute-start(f32[64,512]{1,0:T(8,128)S(1)} %get-tuple-element.18), channel_id=1, source_target_pairs={{0,24},{1,56},{8,33},{9,1},{16,42},{17,10},{24,51},{25,19},{32,60}... | collective-permute-start | bytes 393224 | tf_op jit(solution)/shard_map/ppermute | solution.py:150
  75.2 8.5 %collective-permute-start.3 = (f32[64,512]{1,0:T(8,128)S(1)}, f32[64,512]{1,0:T(8,128)S(1)}, u32[]{:S(2)}, u32[]{:S(2)}) collective-permute-start(f32[64,512]{1,0:T(8,128)S(1)} %get-tuple-element.19), channel_id=1, source_target_pairs={{0,32},{1,0},{8,41},{9,9},{16,50},{17,18},{24,59},{25,27},{32,4},{... | collective-permute-start | bytes 393224 | tf_op jit(solution)/shard_map/ppermute | solution.py:150
  76.6 7.2 %collective-permute-start.2 = (f32[64,512]{1,0:T(8,128)S(1)}, f32[64,512]{1,0:T(8,128)S(1)}, u32[]{:S(2)}, u32[]{:S(2)}) collective-permute-start(f32[64,512]{1,0:T(8,128)S(1)} %get-tuple-element.20), channel_id=1, source_target_pairs={{0,40},{1,8},{8,49},{9,17},{16,58},{17,26},{24,3},{25,35},{32,12},... | collective-permute-start | bytes 393224 | tf_op jit(solution)/shard_map/ppermute | solution.py:150
  79.2 4.5 %collective-permute-start.1 = (f32[64,512]{1,0:T(8,128)S(1)}, f32[64,512]{1,0:T(8,128)S(1)}, u32[]{:S(2)}, u32[]{:S(2)}) collective-permute-start(f32[64,512]{1,0:T(8,128)S(1)} %get-tuple-element.21), channel_id=1, source_target_pairs={{0,48},{1,16},{8,57},{9,25},{16,2},{17,34},{24,11},{25,43},{32,20}... | collective-permute-start | bytes 393224 | tf_op jit(solution)/shard_map/ppermute | solution.py:150
  80.5 4.9 %collective-permute-start = (f32[64,512]{1,0:T(8,128)S(1)}, f32[64,512]{1,0:T(8,128)S(1)}, u32[]{:S(2)}, u32[]{:S(2)}) collective-permute-start(f32[64,512]{1,0:T(8,128)S(1)} %get-tuple-element.22), channel_id=1, source_target_pairs={{0,56},{1,24},{8,1},{9,33},{16,10},{17,42},{24,19},{25,51},{32,28}... | collective-permute-start | bytes 393224 | tf_op jit(solution)/shard_map/ppermute | solution.py:150
  156.6 76.8 %all-to-all-start.2 = ((f32[32,8,2,8,256]{4,3,1,2,0:T(8,128)}), f32[32,8,2,8,256]{4,3,1,2,0:T(8,128)}, u32[]{:S(2)}, u32[]{:S(2)}) async-start(f32[32,8,2,8,256]{4,3,1,2,0:T(8,128)} %broadcast_in_dim.19), calls=%async_computation.2 | async-start | bytes 8388608 | tf_op jit(solution)/shard_map/all_to_all | solution.py:128
  291.4 2.0 copy-start
  298.4 10.2 %copy-start.1 = (f32[1024,1024]{1,0:T(8,128)S(1)}, f32[1024,1024]{1,0:T(8,128)}, u32[]{:S(2)}) copy-start(f32[1024,1024]{1,0:T(8,128)} %copy-done) | copy-start | bytes 12582916
  308.6 8.2 %copy-start.5 = (f32[1024,256]{1,0:T(8,128)S(1)}, f32[1024,256]{1,0:T(8,128)}, u32[]{:S(2)}) copy-start(f32[1024,256]{1,0:T(8,128)} %get-tuple-element.26) | copy-start | bytes 3145732
  308.6 8.2 %copy-start.6 = (f32[512,256]{1,0:T(8,128)S(1)}, f32[512,256]{1,0:T(8,128)}, u32[]{:S(2)}) copy-start(f32[512,256]{1,0:T(8,128)} %param.5) | copy-start | bytes 1572868
  315.5 1.3 copy-start.2
  330.4 2.0 copy-start.3
Sparse Core Ops, SparseCore 0:
  37.0 47.2 all-gather.9
  86.6 43.1 all-gather.5
  132.4 101.4 all-gather.7
